TPU v7x, 32 devices: a whole 2x2x4 slice. The times are simulated.
32 devices in a mesh: tm: 4 (over y, x), space: 8 (over z, core).
Axes of the slice: x: 2, y: 2, z: 4, core: 2. Of those that a mesh axis runs over, the one named last changes fastest.
Arguments:
- speed_sq: float32 [32, 256, 256], P('space'), may hold values from 0.04 to 0.3
- misfit_weight: float32 [32, 256, 256], P('space'), may hold values from 0.1 to 1
- checkpoints: float32 [4, 2, 32, 256, 256], P('tm', None, 'space'), may hold values from -6 to 6
- adjoint_final: float32 [2, 32, 256, 256], P(None, 'space'), may hold values from -6 to 6
- slab_steps: int32 [4], replicated, may hold values from 1 to 6, as said below
- restart_group: int32 [4], replicated, may hold values from 0 to 3, as said below
Outputs:
- gradient_image: float32 [32, 256, 256], P('space')
- adjoint_start: float32 [4, 2, 32, 256, 256], P('tm', None, 'space')
Inputs may be any that keep to these rules, and one draw needn't show every extreme that they name: `slab_steps`: one slab has exactly 6 steps. `restart_group`: each group is named once.
All inputs are finite; a program needn't handle non-finite values.
Results may differ from a plain program's by a relative error of at most 0.00002.
Values sent between devices are 32-bit elements; how exact they have to be, the bound alone decides.
A program may use at most 128 MiB of HBM per device.

v0:
```python
import jax
import jax.numpy as jnp
from jax import lax
from jax.sharding import PartitionSpec as P

SLAB_MAX = 6


def extended(shard, sides, width):
    for axis, dim in sides:
        count, length = (lax.axis_size(axis), shard.shape[dim])
        up = [(i, (i + 1) % count) for i in range(count - 1)]
        down = [(j, i) for i, j in up]
        last = lax.slice_in_dim(shard, length - width, length, axis=dim)
        initial = lax.slice_in_dim(shard, 0, width, axis=dim)
        before = lax.ppermute(last, axis, up)
        after = lax.ppermute(initial, axis, down)
        shard = jnp.concatenate([before, shard, after], axis=dim)
    return shard


def passed_along(value, axis, steps):
    count = lax.axis_size(axis)
    initial, last = (max(0, -steps), min(count, count - steps))
    return lax.ppermute(value, axis, [(source, source + steps) for source in range(initial, last)])


def yz_sum(center):
    padded = jnp.pad(center, ((0, 0), (1, 1), (1, 1)))
    return padded[:, 2:, 1:-1] + padded[:, :-2, 1:-1] + padded[:, 1:-1, 2:] + padded[:, 1:-1, :-2]


def lap_padded(padded):
    center = padded[1:-1]
    return padded[2:] + padded[:-2] + yz_sum(center) - 6.0 * center


def adjoint_lap(field):
    return lap_padded(extended(field, (("space", 0),), 1))


def shards(speed_sq, misfit_weight, checkpoints, adjoint_final, slab_steps, restart_group):
    group = lax.axis_index("tm")
    count = lax.axis_size("tm")
    length = lax.dynamic_index_in_dim(slab_steps, group, 0, keepdims=False)
    source = lax.dynamic_index_in_dim(restart_group, group, 0, keepdims=False)
    stored = lax.all_gather(checkpoints, "tm", axis=0, tiled=True)
    restart = lax.dynamic_index_in_dim(stored, source, 0, keepdims=False)
    previous, current = (restart[0], restart[1])
    fields = [current]
    laplaces = []
    for step_at in range(SLAB_MAX):
        laplace = lap_padded(extended(current, (("space", 0),), 1))
        following = 2.0 * current - previous + speed_sq * laplace
        laplaces.append(laplace)
        fields.append(following)
        previous, current = (current, following)
    fields = jnp.stack(fields)
    laplaces = jnp.stack(laplaces)

    def one_step(turn_step, carry):
        adj_now, adj_next, image = carry
        step_at = length - turn_step
        active = step_at >= 1
        field_now = lax.dynamic_index_in_dim(
            fields, jnp.clip(step_at, 0, SLAB_MAX), 0, keepdims=False
        )
        lap_before = lax.dynamic_index_in_dim(
            laplaces, jnp.clip(step_at - 1, 0, SLAB_MAX - 1), 0, keepdims=False
        )
        adj_prev = (
            2.0 * adj_now - adj_next + adjoint_lap(speed_sq * adj_now) + misfit_weight * field_now
        )
        image = image + jnp.where(active, adj_now * lap_before, jnp.zeros_like(adj_now))
        return (jnp.where(active, adj_prev, adj_now), jnp.where(active, adj_now, adj_next), image)

    is_last = group == count - 1
    carry_in = jnp.where(is_last, adjoint_final, jnp.zeros_like(adjoint_final))
    image = jnp.zeros_like(speed_sq)
    start_pair = carry_in
    for turn in range(count):
        adj_now, adj_next, image = lax.fori_loop(
            0, SLAB_MAX, one_step, (carry_in[0], carry_in[1], jnp.zeros_like(speed_sq))
        )
        start_pair = jnp.stack([adj_now, adj_next])
        if turn + 1 < count:
            passed = passed_along(start_pair, "tm", -1)
            carry_in = jnp.where(is_last, adjoint_final, passed)
    total = lax.psum(image, "tm")
    return (total, start_pair[None])


def solution(mesh):
    placed = (
        P("space", None, None),
        P("space", None, None),
        P("tm", None, "space", None, None),
        P(None, "space", None, None),
        P(),
        P(),
    )
    return jax.shard_map(
        shards,
        mesh=mesh,
        in_specs=placed,
        out_specs=(P("space", None, None), P("tm", None, "space", None, None)),
        check_vma=False,
    )
```

profile of v0, /device:TPU:0, one launch (start us, length us, event | category | flops | bytes accessed | tf_op | source)
XLA Modules:
  0.0 807.3 jit_solution(9377997287016560706)
XLA Ops:
  10.5 89.7 %all-gather.2.cloned.1.call-done = f32[4,2,4,256,256]{4,3,2,1,0:T(8,128)} async-done(((f32[1,2,4,256,256]{4,3,2,1,0:T(8,128)}), f32[4,2,4,256,256]{4,3,2,1,0:T(8,128)}) %all-gather.2.cloned.1.call-update) | async-done | bytes 8388624 | tf_op jit(solution)/shard_map/all_gather | solution.py:47
  124.0 6.4 collective-permute-start.13
  137.3 7.9 collective-permute-start.15
  151.1 7.2 collective-permute-start.17
  163.7 7.2 collective-permute-start.19
  175.4 99.2 %while.71 = (s32[]{:T(128)}, f32[4,256,256]{2,1,0:T(8,128)}, f32[4,256,256]{2,1,0:T(8,128)}, s32[]{:T(128)}, f32[4,256,256]{2,1,0:T(8,128)S(1)}, /*index=5*/f32[...) while((s32[]{:T(128)}, f32[4,256,256]{2,1,0:T(8,128)}, ...), condition=%wide.region_1.2_spmd, body=%wide.region_0.1_spmd.sunk | while | flops 4456454 | bytes 14156007 | solution.py:82
  195.7 6.6 collective-permute-start
  212.3 6.1 collective-permute-start
  228.4 6.1 collective-permute-start
  244.6 6.1 collective-permute-start
  260.7 6.1 collective-permute-start
  278.9 46.1 %collective-permute-done.20 = f32[2,4,256,256]{3,2,1,0:T(8,128)} collective-permute-done((f32[2,4,256,256]{3,2,1,0:T(8,128)}, f32[2,4,256,256]{3,2,1,0:T(8,128)}, u32[]{:S(2)}, u32[]{:S(2)}) %collective-permute-start.20) | collective-permute-done | bytes 2097184 | tf_op jit(solution)/shard_map/ppermute | solution.py:25
  328.5 99.2 %while.72 = (s32[]{:T(128)}, f32[4,256,256]{2,1,0:T(8,128)}, f32[4,256,256]{2,1,0:T(8,128)}, s32[]{:T(128)}, f32[4,256,256]{2,1,0:T(8,128)S(1)}, /*index=5*/f32[...) while((s32[]{:T(128)}, f32[4,256,256]{2,1,0:T(8,128)}, ...), condition=%wide.region_3.4_spmd, body=%wide.region_2.3_spmd.sunk | while | flops 4456454 | bytes 14156007 | solution.py:82
  348.7 6.6 collective-permute-start.2
  365.4 6.1 collective-permute-start.2
  381.5 6.1 collective-permute-start.2
  397.6 6.1 collective-permute-start.2
  413.7 6.1 collective-permute-start.2
  432.2 46.0 %collective-permute-done.21 = f32[2,4,256,256]{3,2,1,0:T(8,128)} collective-permute-done((f32[2,4,256,256]{3,2,1,0:T(8,128)}, f32[2,4,256,256]{3,2,1,0:T(8,128)}, u32[]{:S(2)}, u32[]{:S(2)}) %collective-permute-start.21) | collective-permute-done | bytes 2097184 | tf_op jit(solution)/shard_map/ppermute | solution.py:25
  481.6 100.0 %while.73 = (s32[]{:T(128)}, f32[4,256,256]{2,1,0:T(8,128)}, f32[4,256,256]{2,1,0:T(8,128)}, s32[]{:T(128)}, f32[4,256,256]{2,1,0:T(8,128)S(1)}, /*index=5*/f32[...) while((s32[]{:T(128)}, f32[4,256,256]{2,1,0:T(8,128)}, ...), condition=%wide.region_5.6_spmd, body=%wide.region_4.5_spmd.sunk | while | flops 4456454 | bytes 14156007 | solution.py:82
  501.8 6.6 collective-permute-start.4
  518.4 7.0 collective-permute-start.4
  535.4 6.1 collective-permute-start.4
  551.6 6.1 collective-permute-start.4
  585.9 46.5 %collective-permute-done.22 = f32[2,4,256,256]{3,2,1,0:T(8,128)} collective-permute-done((f32[2,4,256,256]{3,2,1,0:T(8,128)}, f32[2,4,256,256]{3,2,1,0:T(8,128)}, u32[]{:S(2)}, u32[]{:S(2)}) %collective-permute-start.22) | collective-permute-done | bytes 2097184 | tf_op jit(solution)/shard_map/ppermute | solution.py:25
  636.0 106.2 %while.74 = (s32[]{:T(128)}, f32[4,256,256]{2,1,0:T(8,128)}, f32[4,256,256]{2,1,0:T(8,128)}, f32[4,256,256]{2,1,0:T(8,128)}, s32[]{:T(128)}, /*index=5*/f32[4,25...) while((s32[]{:T(128)}, f32[4,256,256]{2,1,0:T(8,128)}, ...), condition=%wide.region_7.8_spmd.clone, body=%wide.region_6.7_spmd.clone.sunk | while | flops 5505034 | bytes 17301816 | solution.py:82
  656.8 6.6 collective-permute-start.6
  674.6 6.8 collective-permute-start.6
  692.5 6.1 collective-permute-start.6
  709.8 6.1 collective-permute-start.6
  727.0 6.1 collective-permute-start.6
  745.2 53.0 %all-reduce.12.cloned.1.call-done = f32[4,256,256]{2,1,0:T(8,128)} async-done(((f32[4,256,256]{2,1,0:T(8,128)}), f32[4,256,256]{2,1,0:T(8,128)}) %all-reduce.12.cloned.1.call-update) | async-done | bytes 1048592 | tf_op jit(solution)/shard_map/psum | solution.py:89
  (224 shorter events, 345.2 us)
Async XLA Ops:
  7.2 93.0 %all-gather.2.cloned.1.call-start = ((), (), s32[]{:S(2)}) async-start(), calls=%async_computation | async-start | bytes 10485760 | tf_op jit(solution)/shard_map/all_gather | solution.py:47
  7.9 790.3 %all-reduce.12.cloned.1.call-start = ((), (), s32[]{:S(2)}) async-start(), calls=%async_computation.1 | async-start | bytes 2097152 | tf_op jit(solution)/shard_map/psum | solution.py:89
  136.0 9.8 %collective-permute-start.14 = (f32[1,256,256]{2,1,0:T(8,128)}, f32[1,256,256]{2,1,0:T(8,128)S(1)}, u32[]{:S(2)}, u32[]{:S(2)}) collective-permute-start(f32[1,256,256]{2,1,0:T(8,128)} %get-tuple-element.908), channel_id=1, source_target_pairs={{1,0},{2,1},{3,2},{4,3},{5,4},{6,5},{7,6},{9,8},{10,9},{11,10},{12... | collective-permute-start | bytes 786440 | tf_op jit(solution)/shard_map/ppermute | solution.py:17
  137.3 8.7 %collective-permute-start.15 = (f32[1,256,256]{2,1,0:T(8,128)}, f32[1,256,256]{2,1,0:T(8,128)}, u32[]{:S(2)}, u32[]{:S(2)}) collective-permute-start(f32[1,256,256]{2,1,0:T(8,128)} %get-tuple-element.909), channel_id=1, source_target_pairs={{0,1},{1,2},{2,3},{3,4},{4,5},{5,6},{6,7},{8,9},{9,10},{10,11},{11... | collective-permute-start | bytes 786440 | tf_op jit(solution)/shard_map/ppermute | solution.py:16
  149.8 8.7 %collective-permute-start.16 = (f32[1,256,256]{2,1,0:T(8,128)S(1)}, f32[1,256,256]{2,1,0:T(8,128)S(1)}, u32[]{:S(2)}, u32[]{:S(2)}) collective-permute-start(f32[1,256,256]{2,1,0:T(8,128)S(1)} %get-tuple-element.906), channel_id=1, source_target_pairs={{1,0},{2,1},{3,2},{4,3},{5,4},{6,5},{7,6},{9,8},{10,9},{11,10},{12... | collective-permute-start | bytes 786440 | tf_op jit(solution)/shard_map/ppermute | solution.py:17
  151.1 8.3 %collective-permute-start.17 = (f32[1,256,256]{2,1,0:T(8,128)S(1)}, f32[1,256,256]{2,1,0:T(8,128)S(1)}, u32[]{:S(2)}, u32[]{:S(2)}) collective-permute-start(f32[1,256,256]{2,1,0:T(8,128)S(1)} %get-tuple-element.907), channel_id=1, source_target_pairs={{0,1},{1,2},{2,3},{3,4},{4,5},{5,6},{6,7},{8,9},{9,10},{10,11},{11... | collective-permute-start | bytes 786440 | tf_op jit(solution)/shard_map/ppermute | solution.py:16
  162.4 10.0 %collective-permute-start.18 = (f32[1,256,256]{2,1,0:T(8,128)S(1)}, f32[1,256,256]{2,1,0:T(8,128)S(1)}, u32[]{:S(2)}, u32[]{:S(2)}) collective-permute-start(f32[1,256,256]{2,1,0:T(8,128)S(1)} %get-tuple-element.904), channel_id=1, source_target_pairs={{1,0},{2,1},{3,2},{4,3},{5,4},{6,5},{7,6},{9,8},{10,9},{11,10},{12... | collective-permute-start | bytes 786440 | tf_op jit(solution)/shard_map/ppermute | solution.py:17
  163.7 8.7 %collective-permute-start.19 = (f32[1,256,256]{2,1,0:T(8,128)S(1)}, f32[1,256,256]{2,1,0:T(8,128)S(1)}, u32[]{:S(2)}, u32[]{:S(2)}) collective-permute-start(f32[1,256,256]{2,1,0:T(8,128)S(1)} %get-tuple-element.905), channel_id=1, source_target_pairs={{0,1},{1,2},{2,3},{3,4},{4,5},{5,6},{6,7},{8,9},{9,10},{10,11},{11... | collective-permute-start | bytes 786440 | tf_op jit(solution)/shard_map/ppermute | solution.py:16
  177.6 8.1 collective-permute-start
  195.7 8.6 %collective-permute-start = (f32[1,256,256]{2,1,0:T(8,128)}, f32[1,256,256]{2,1,0:T(8,128)S(1)}, u32[]{:S(2)}, u32[]{:S(2)}) collective-permute-start(f32[1,256,256]{2,1,0:T(8,128)} %get-tuple-element.1092), channel_id=1, source_target_pairs={{0,1},{1,2},{2,3},{3,4},{4,5},{5,6},{6,7},{8,9},{9,10},{10,11},{11... | collective-permute-start | bytes 786440 | tf_op jit(solution)/shard_map/while/body/eval_jaxpr/ppermute | solution.py:16
  212.3 8.1 %collective-permute-start = (f32[1,256,256]{2,1,0:T(8,128)}, f32[1,256,256]{2,1,0:T(8,128)S(1)}, u32[]{:S(2)}, u32[]{:S(2)}) collective-permute-start(f32[1,256,256]{2,1,0:T(8,128)} %get-tuple-element.1092), channel_id=1, source_target_pairs={{0,1},{1,2},{2,3},{3,4},{4,5},{5,6},{6,7},{8,9},{9,10},{10,11},{11... | collective-permute-start | bytes 786440 | tf_op jit(solution)/shard_map/while/body/eval_jaxpr/ppermute | solution.py:16
  228.4 8.1 %collective-permute-start = (f32[1,256,256]{2,1,0:T(8,128)}, f32[1,256,256]{2,1,0:T(8,128)S(1)}, u32[]{:S(2)}, u32[]{:S(2)}) collective-permute-start(f32[1,256,256]{2,1,0:T(8,128)} %get-tuple-element.1092), channel_id=1, source_target_pairs={{0,1},{1,2},{2,3},{3,4},{4,5},{5,6},{6,7},{8,9},{9,10},{10,11},{11... | collective-permute-start | bytes 786440 | tf_op jit(solution)/shard_map/while/body/eval_jaxpr/ppermute | solution.py:16
  244.6 8.1 %collective-permute-start = (f32[1,256,256]{2,1,0:T(8,128)}, f32[1,256,256]{2,1,0:T(8,128)S(1)}, u32[]{:S(2)}, u32[]{:S(2)}) collective-permute-start(f32[1,256,256]{2,1,0:T(8,128)} %get-tuple-element.1092), channel_id=1, source_target_pairs={{0,1},{1,2},{2,3},{3,4},{4,5},{5,6},{6,7},{8,9},{9,10},{10,11},{11... | collective-permute-start | bytes 786440 | tf_op jit(solution)/shard_map/while/body/eval_jaxpr/ppermute | solution.py:16
  260.7 8.1 %collective-permute-start = (f32[1,256,256]{2,1,0:T(8,128)}, f32[1,256,256]{2,1,0:T(8,128)S(1)}, u32[]{:S(2)}, u32[]{:S(2)}) collective-permute-start(f32[1,256,256]{2,1,0:T(8,128)} %get-tuple-element.1092), channel_id=1, source_target_pairs={{0,1},{1,2},{2,3},{3,4},{4,5},{5,6},{6,7},{8,9},{9,10},{10,11},{11... | collective-permute-start | bytes 786440 | tf_op jit(solution)/shard_map/while/body/eval_jaxpr/ppermute | solution.py:16
  277.6 47.4 %collective-permute-start.20 = (f32[2,4,256,256]{3,2,1,0:T(8,128)}, f32[2,4,256,256]{3,2,1,0:T(8,128)}, u32[]{:S(2)}, u32[]{:S(2)}) collective-permute-start(f32[2,4,256,256]{3,2,1,0:T(8,128)} %pad_maximum_fusion.8), channel_id=1, source_target_pairs={{8,0},{16,8},{24,16},{9,1},{17,9},{25,17},{10,2},{18,10},{26,18},{... | collective-permute-start | bytes 6291464 | tf_op jit(solution)/shard_map/ppermute | solution.py:25
  348.7 8.6 %collective-permute-start.2 = (f32[1,256,256]{2,1,0:T(8,128)}, f32[1,256,256]{2,1,0:T(8,128)S(1)}, u32[]{:S(2)}, u32[]{:S(2)}) collective-permute-start(f32[1,256,256]{2,1,0:T(8,128)} %get-tuple-element.1103), channel_id=1, source_target_pairs={{0,1},{1,2},{2,3},{3,4},{4,5},{5,6},{6,7},{8,9},{9,10},{10,11},{11... | collective-permute-start | bytes 786440 | tf_op jit(solution)/shard_map/while/body/eval_jaxpr/ppermute | solution.py:16
  365.4 8.1 %collective-permute-start.2 = (f32[1,256,256]{2,1,0:T(8,128)}, f32[1,256,256]{2,1,0:T(8,128)S(1)}, u32[]{:S(2)}, u32[]{:S(2)}) collective-permute-start(f32[1,256,256]{2,1,0:T(8,128)} %get-tuple-element.1103), channel_id=1, source_target_pairs={{0,1},{1,2},{2,3},{3,4},{4,5},{5,6},{6,7},{8,9},{9,10},{10,11},{11... | collective-permute-start | bytes 786440 | tf_op jit(solution)/shard_map/while/body/eval_jaxpr/ppermute | solution.py:16
  381.5 8.1 %collective-permute-start.2 = (f32[1,256,256]{2,1,0:T(8,128)}, f32[1,256,256]{2,1,0:T(8,128)S(1)}, u32[]{:S(2)}, u32[]{:S(2)}) collective-permute-start(f32[1,256,256]{2,1,0:T(8,128)} %get-tuple-element.1103), channel_id=1, source_target_pairs={{0,1},{1,2},{2,3},{3,4},{4,5},{5,6},{6,7},{8,9},{9,10},{10,11},{11... | collective-permute-start | bytes 786440 | tf_op jit(solution)/shard_map/while/body/eval_jaxpr/ppermute | solution.py:16
  397.6 8.1 %collective-permute-start.2 = (f32[1,256,256]{2,1,0:T(8,128)}, f32[1,256,256]{2,1,0:T(8,128)S(1)}, u32[]{:S(2)}, u32[]{:S(2)}) collective-permute-start(f32[1,256,256]{2,1,0:T(8,128)} %get-tuple-element.1103), channel_id=1, source_target_pairs={{0,1},{1,2},{2,3},{3,4},{4,5},{5,6},{6,7},{8,9},{9,10},{10,11},{11... | collective-permute-start | bytes 786440 | tf_op jit(solution)/shard_map/while/body/eval_jaxpr/ppermute | solution.py:16
  413.7 8.1 %collective-permute-start.2 = (f32[1,256,256]{2,1,0:T(8,128)}, f32[1,256,256]{2,1,0:T(8,128)S(1)}, u32[]{:S(2)}, u32[]{:S(2)}) collective-permute-start(f32[1,256,256]{2,1,0:T(8,128)} %get-tuple-element.1103), channel_id=1, source_target_pairs={{0,1},{1,2},{2,3},{3,4},{4,5},{5,6},{6,7},{8,9},{9,10},{10,11},{11... | collective-permute-start | bytes 786440 | tf_op jit(solution)/shard_map/while/body/eval_jaxpr/ppermute | solution.py:16
  430.7 47.4 %collective-permute-start.21 = (f32[2,4,256,256]{3,2,1,0:T(8,128)}, f32[2,4,256,256]{3,2,1,0:T(8,128)}, u32[]{:S(2)}, u32[]{:S(2)}) collective-permute-start(f32[2,4,256,256]{3,2,1,0:T(8,128)} %pad_maximum_fusion.9), channel_id=1, source_target_pairs={{8,0},{16,8},{24,16},{9,1},{17,9},{25,17},{10,2},{18,10},{26,18},{... | collective-permute-start | bytes 6291464 | tf_op jit(solution)/shard_map/ppermute | solution.py:25
  501.8 8.6 %collective-permute-start.4 = (f32[1,256,256]{2,1,0:T(8,128)}, f32[1,256,256]{2,1,0:T(8,128)S(1)}, u32[]{:S(2)}, u32[]{:S(2)}) collective-permute-start(f32[1,256,256]{2,1,0:T(8,128)} %get-tuple-element.1114), channel_id=1, source_target_pairs={{0,1},{1,2},{2,3},{3,4},{4,5},{5,6},{6,7},{8,9},{9,10},{10,11},{11... | collective-permute-start | bytes 786440 | tf_op jit(solution)/shard_map/while/body/eval_jaxpr/ppermute | solution.py:16
  518.4 8.9 %collective-permute-start.4 = (f32[1,256,256]{2,1,0:T(8,128)}, f32[1,256,256]{2,1,0:T(8,128)S(1)}, u32[]{:S(2)}, u32[]{:S(2)}) collective-permute-start(f32[1,256,256]{2,1,0:T(8,128)} %get-tuple-element.1114), channel_id=1, source_target_pairs={{0,1},{1,2},{2,3},{3,4},{4,5},{5,6},{6,7},{8,9},{9,10},{10,11},{11... | collective-permute-start | bytes 786440 | tf_op jit(solution)/shard_map/while/body/eval_jaxpr/ppermute | solution.py:16
  535.4 8.1 %collective-permute-start.4 = (f32[1,256,256]{2,1,0:T(8,128)}, f32[1,256,256]{2,1,0:T(8,128)S(1)}, u32[]{:S(2)}, u32[]{:S(2)}) collective-permute-start(f32[1,256,256]{2,1,0:T(8,128)} %get-tuple-element.1114), channel_id=1, source_target_pairs={{0,1},{1,2},{2,3},{3,4},{4,5},{5,6},{6,7},{8,9},{9,10},{10,11},{11... | collective-permute-start | bytes 786440 | tf_op jit(solution)/shard_map/while/body/eval_jaxpr/ppermute | solution.py:16
  551.6 8.1 %collective-permute-start.4 = (f32[1,256,256]{2,1,0:T(8,128)}, f32[1,256,256]{2,1,0:T(8,128)S(1)}, u32[]{:S(2)}, u32[]{:S(2)}) collective-permute-start(f32[1,256,256]{2,1,0:T(8,128)} %get-tuple-element.1114), channel_id=1, source_target_pairs={{0,1},{1,2},{2,3},{3,4},{4,5},{5,6},{6,7},{8,9},{9,10},{10,11},{11... | collective-permute-start | bytes 786440 | tf_op jit(solution)/shard_map/while/body/eval_jaxpr/ppermute | solution.py:16
  567.7 8.1 %collective-permute-start.4 = (f32[1,256,256]{2,1,0:T(8,128)}, f32[1,256,256]{2,1,0:T(8,128)S(1)}, u32[]{:S(2)}, u32[]{:S(2)}) collective-permute-start(f32[1,256,256]{2,1,0:T(8,128)} %get-tuple-element.1114), channel_id=1, source_target_pairs={{0,1},{1,2},{2,3},{3,4},{4,5},{5,6},{6,7},{8,9},{9,10},{10,11},{11... | collective-permute-start | bytes 786440 | tf_op jit(solution)/shard_map/while/body/eval_jaxpr/ppermute | solution.py:16
  584.6 47.8 %collective-permute-start.22 = (f32[2,4,256,256]{3,2,1,0:T(8,128)}, f32[2,4,256,256]{3,2,1,0:T(8,128)}, u32[]{:S(2)}, u32[]{:S(2)}) collective-permute-start(f32[2,4,256,256]{3,2,1,0:T(8,128)} %pad_maximum_fusion.10), channel_id=1, source_target_pairs={{8,0},{16,8},{24,16},{9,1},{17,9},{25,17},{10,2},{18,10},{26,18},{... | collective-permute-start | bytes 6291464 | tf_op jit(solution)/shard_map/ppermute | solution.py:25
  656.8 8.6 %collective-permute-start.6 = (f32[1,256,256]{2,1,0:T(8,128)}, f32[1,256,256]{2,1,0:T(8,128)S(1)}, u32[]{:S(2)}, u32[]{:S(2)}) collective-permute-start(f32[1,256,256]{2,1,0:T(8,128)} %get-tuple-element.1127), channel_id=1, source_target_pairs={{0,1},{1,2},{2,3},{3,4},{4,5},{5,6},{6,7},{8,9},{9,10},{10,11},{11... | collective-permute-start | bytes 786440 | tf_op jit(solution)/shard_map/while/body/eval_jaxpr/ppermute | solution.py:16
  674.6 8.7 %collective-permute-start.6 = (f32[1,256,256]{2,1,0:T(8,128)}, f32[1,256,256]{2,1,0:T(8,128)S(1)}, u32[]{:S(2)}, u32[]{:S(2)}) collective-permute-start(f32[1,256,256]{2,1,0:T(8,128)} %get-tuple-element.1127), channel_id=1, source_target_pairs={{0,1},{1,2},{2,3},{3,4},{4,5},{5,6},{6,7},{8,9},{9,10},{10,11},{11... | collective-permute-start | bytes 786440 | tf_op jit(solution)/shard_map/while/body/eval_jaxpr/ppermute | solution.py:16
  692.5 8.1 %collective-permute-start.6 = (f32[1,256,256]{2,1,0:T(8,128)}, f32[1,256,256]{2,1,0:T(8,128)S(1)}, u32[]{:S(2)}, u32[]{:S(2)}) collective-permute-start(f32[1,256,256]{2,1,0:T(8,128)} %get-tuple-element.1127), channel_id=1, source_target_pairs={{0,1},{1,2},{2,3},{3,4},{4,5},{5,6},{6,7},{8,9},{9,10},{10,11},{11... | collective-permute-start | bytes 786440 | tf_op jit(solution)/shard_map/while/body/eval_jaxpr/ppermute | solution.py:16
  709.8 8.1 %collective-permute-start.6 = (f32[1,256,256]{2,1,0:T(8,128)}, f32[1,256,256]{2,1,0:T(8,128)S(1)}, u32[]{:S(2)}, u32[]{:S(2)}) collective-permute-start(f32[1,256,256]{2,1,0:T(8,128)} %get-tuple-element.1127), channel_id=1, source_target_pairs={{0,1},{1,2},{2,3},{3,4},{4,5},{5,6},{6,7},{8,9},{9,10},{10,11},{11... | collective-permute-start | bytes 786440 | tf_op jit(solution)/shard_map/while/body/eval_jaxpr/ppermute | solution.py:16
  727.0 8.1 %collective-permute-start.6 = (f32[1,256,256]{2,1,0:T(8,128)}, f32[1,256,256]{2,1,0:T(8,128)S(1)}, u32[]{:S(2)}, u32[]{:S(2)}) collective-permute-start(f32[1,256,256]{2,1,0:T(8,128)} %get-tuple-element.1127), channel_id=1, source_target_pairs={{0,1},{1,2},{2,3},{3,4},{4,5},{5,6},{6,7},{8,9},{9,10},{10,11},{11... | collective-permute-start | bytes 786440 | tf_op jit(solution)/shard_map/while/body/eval_jaxpr/ppermute | solution.py:16
  (39 other events, 191.0 us)
Sparse Core Ops, SparseCore 0:
  9.9 90.2 all-gather.1
  742.3 55.8 all-reduce.11
where the time goes:
time: 811 us; the launch traced here: 807 us
  waiting for transfers between devices  340 us (42%)
  starting transfers between devices  226 us (28%)
  other arithmetic  172 us (21%)
  local copies, waits for them, and re-layouts  37 us (5%)
  between operations  16.3 us (2%)
  loops' own time  15.7 us (2%)
    ppermute x30, starting transfers between devices, extended(): before = lax.ppermute(last, axis, up)  184 us
    ppermute x3, waiting for transfers between devices, passed_along(): lax.ppermute(value, axis, [(source, source + steps) for source in range(i...  139 us
    select_n x24, other arithmetic, one_step(): jnp.where(active, adj_now, adj_next)  103 us
    all_gather x1, waiting for transfers between devices, shards(): stored = lax.all_gather(checkpoints, 'tm', axis=0, tiled=True)  89.7 us
    ppermute x30, waiting for transfers between devices, extended(): after = lax.ppermute(initial, axis, down)  54.2 us
    psum x1, waiting for transfers between devices, shards(): total = lax.psum(image, 'tm')  53 us
    ppermute x30, starting transfers between devices, extended(): after = lax.ppermute(initial, axis, down)  38.8 us
    mul x24, other arithmetic, one_step(): speed_sq * adj_now  32.6 us
  transfers between devices with their start and end apart: 65, of which 33 were waited for; matrix products, arithmetic and copies ran while one was open for 1% of the time, Pallas kernels for 0%

commit v1 on v0

v1 whole, which is shorter than its diff:
```python
import functools

import jax
import jax.numpy as jnp
from jax import lax
from jax.experimental import pallas as pl
from jax.experimental.pallas import tpu as pltpu
from jax.sharding import PartitionSpec as P

SLAB_MAX = 6
CHUNK = 32
EDGE = 8


def kernel(steps, tab, speed_h, weight_h, ck_h, af_h, img_o, st_o,
           ck, u, laps, s, hist, image, spd, wgt, stage,
           load_sem, ck_send, ck_recv, f_send, f_recv, a_send, a_recv,
           st_send, st_recv, im_send, im_recv):
    groups = st_recv.shape[0]
    planes, rows, _ = spd.shape
    me = lax.axis_index("tm")
    sp = lax.axis_index("space")
    n_tm = lax.axis_size("tm")
    n_sp = lax.axis_size("space")

    def place(m):
        return m + (m // 2) * (1 - 2 * (m % 2))

    q = place(me)
    inner = pl.ds(EDGE, rows)
    span = pl.ds(1, planes)
    partners = [lax.rem(me + d, n_tm) for d in range(1, n_tm)]
    has = [sp > 0, sp < n_sp - 1, q > 0, q < n_tm - 1]
    opposite = [1, 0, 3, 2]
    target = [{"space": jnp.maximum(sp - 1, 0)}, {"space": jnp.minimum(sp + 1, n_sp - 1)},
              {"tm": place(jnp.maximum(q - 1, 0))}, {"tm": place(jnp.minimum(q + 1, n_tm - 1))}]

    def halo(d, ref, at, send, recv):
        if d == 0:
            src, dst = ref.at[at, 1, inner, :], ref.at[at, planes + 1, inner, :]
        elif d == 1:
            src, dst = ref.at[at, planes, inner, :], ref.at[at, 0, inner, :]
        elif d == 2:
            src, dst = ref.at[at, span, pl.ds(EDGE, EDGE), :], ref.at[at, span, pl.ds(EDGE + rows, EDGE), :]
        else:
            src, dst = ref.at[at, span, pl.ds(rows, EDGE), :], ref.at[at, span, pl.ds(0, EDGE), :]
        return pltpu.make_async_remote_copy(
            src_ref=src, dst_ref=dst, send_sem=send, recv_sem=recv,
            device_id=target[d], device_id_type=pl.DeviceIdType.MESH)

    def start(dirs, ref, at, sems):
        for d in dirs:
            @pl.when(has[d])
            def _():
                halo(d, ref, at, sems[0](d), sems[1](d)).start()

    def finish(ref, at, sems):
        for d in range(4):
            @pl.when(has[opposite[d]])
            def _():
                halo(d, ref, at, sems[0](d), sems[1](d)).wait_recv()
        for d in range(4):
            @pl.when(has[d])
            def _():
                halo(d, ref, at, sems[0](d), sems[1](d)).wait_send()

    mine = pl.ds(pl.multiple_of(q * rows, rows), rows)
    loads = [
        pltpu.make_async_copy(speed_h.at[:, mine, :], spd, load_sem.at[0]),
        pltpu.make_async_copy(weight_h.at[:, mine, :], wgt, load_sem.at[1]),
        pltpu.make_async_copy(af_h.at[0, :, mine, :], hist.at[1], load_sem.at[2]),
        pltpu.make_async_copy(af_h.at[1, :, mine, :], hist.at[0], load_sem.at[3]),
        pltpu.make_async_copy(ck_h.at[0, :, :, mine, :], ck.at[me], load_sem.at[4]),
    ]
    for one in loads:
        one.start()

    barrier = pltpu.get_barrier_semaphore()
    for m in partners:
        pl.semaphore_signal(barrier, inc=1, device_id={"tm": m}, device_id_type=pl.DeviceIdType.MESH)
    for d in range(2):
        @pl.when(has[d])
        def _():
            pl.semaphore_signal(barrier, inc=1, device_id=target[d], device_id_type=pl.DeviceIdType.MESH)
    peers = len(partners) + has[0].astype(jnp.int32) + has[1].astype(jnp.int32)
    pl.semaphore_wait(barrier, peers)

    def ck_copy(i):
        m = partners[i]
        theirs = pl.ds(pl.multiple_of(place(m) * rows, rows), rows)
        return pltpu.make_async_remote_copy(
            src_ref=ck_h.at[0, :, :, theirs, :], dst_ref=ck.at[me],
            send_sem=ck_send.at[i], recv_sem=ck_recv.at[i],
            device_id={"tm": m}, device_id_type=pl.DeviceIdType.MESH)

    for i in range(len(partners)):
        ck_copy(i).start()

    line = jnp.zeros((rows, spd.shape[2]), jnp.float32)
    band = jnp.zeros((EDGE, spd.shape[2]), jnp.float32)
    for ref in (u, s):
        for d, p in ((0, 0), (1, planes + 1)):
            @pl.when(jnp.logical_not(has[d]))
            def _():
                def clear(i, c):
                    ref[i, p, EDGE:EDGE + rows, :] = line
                    return c
                lax.fori_loop(0, ref.shape[0], clear, 0)
        for d, r in ((2, 0), (3, EDGE + rows)):
            @pl.when(jnp.logical_not(has[d]))
            def _():
                def clear(i, c):
                    for p in range(planes):
                        ref[i, 1 + p, r:r + EDGE, :] = band
                    return c
                lax.fori_loop(0, ref.shape[0], clear, 0)
    blank = laps.shape[0] - 1
    for p in range(planes):
        laps[blank, p] = line
        image[p] = line

    lane = lax.broadcasted_iota(jnp.int32, (CHUNK, spd.shape[2]), 1)
    first = lane == 0
    last = lane == spd.shape[2] - 1
    zero = jnp.zeros((CHUNK, spd.shape[2]), jnp.float32)

    def lap(ref, at, p, r):
        c = ref[at, p + 1, EDGE + r:EDGE + r + CHUNK, :]
        total = ref[at, p, EDGE + r:EDGE + r + CHUNK, :] + ref[at, p + 2, EDGE + r:EDGE + r + CHUNK, :]
        total += ref[at, p + 1, EDGE + r - 1:EDGE + r - 1 + CHUNK, :]
        total += ref[at, p + 1, EDGE + r + 1:EDGE + r + 1 + CHUNK, :]
        total += jnp.where(first, zero, pltpu.roll(c, 1, 1))
        total += jnp.where(last, zero, pltpu.roll(c, c.shape[1] - 1, 1))
        return c, total - 6.0 * c

    for one in loads:
        one.wait()

    def a_sems(par):
        return (lambda d: a_send.at[par, d]), (lambda d: a_recv.at[par, d])

    def f_sems(par, g):
        return (lambda d: f_send.at[par, g, d]), (lambda d: f_recv.at[par, g, d])

    for p in range(planes):
        s[0, 1 + p, EDGE:EDGE + rows, :] = spd[p] * hist[1, p]

    for i in range(len(partners)):
        ck_copy(i).wait_recv()
    for g in range(groups):
        source = tab[2 * steps + g]
        for p in range(planes):
            u[groups + g, 1 + p, EDGE:EDGE + rows, :] = ck[source, 1, p]
        start(range(4), u, groups + g, f_sems(0, g))
        for p in range(planes):
            u[g, 1 + p, EDGE:EDGE + rows, :] = ck[source, 0, p]
    start(range(4), s, 0, a_sems(0))

    order = (0, planes - 1) + tuple(range(1, planes - 1))

    def forward(n, carry):
        par, later = lax.rem(n, 2), lax.rem(n + 1, 2)
        for g in range(groups):
            at = (n + 1) * groups + g
            finish(u, at, f_sems(par, g))
            for k, p in enumerate(order):
                for r in range(0, rows, CHUNK):
                    here = slice(EDGE + r, EDGE + r + CHUNK)
                    c, laplace = lap(u, at, p, r)
                    laps[n * groups + g, p, r:r + CHUNK, :] = laplace
                    u[at + groups, 1 + p, here, :] = (
                        2.0 * c - u[at - groups, 1 + p, here, :] + spd[p, r:r + CHUNK, :] * laplace)
                if k == 1:
                    @pl.when(n < SLAB_MAX - 1)
                    def _():
                        start((0, 1), u, at + groups, f_sems(later, g))

            @pl.when(n < SLAB_MAX - 1)
            def _():
                start((2, 3), u, at + groups, f_sems(later, g))
        return carry

    lax.fori_loop(0, SLAB_MAX, forward, 0)

    def adjoint(t, carry):
        par, later = lax.rem(t, 2), lax.rem(t + 1, 2)
        at_u, at_lap = tab[t], tab[steps + t]
        finish(s, par, a_sems(par))
        for k, p in enumerate(order):
            for r in range(0, rows, CHUNK):
                here = slice(r, r + CHUNK)
                pad = slice(EDGE + r, EDGE + r + CHUNK)
                _, laplace = lap(s, par, p, r)
                new = (2.0 * hist[t + 1, p, here, :] - hist[t, p, here, :] + laplace
                       + wgt[p, here, :] * u[at_u, 1 + p, pad, :])
                hist[t + 2, p, here, :] = new
                s[later, 1 + p, pad, :] = spd[p, here, :] * new
            if k == 1:
                @pl.when(t < steps - 1)
                def _():
                    start((0, 1), s, later, a_sems(later))

        @pl.when(t < steps - 1)
        def _():
            start((2, 3), s, later, a_sems(later))
        for p in range(planes):
            for r in range(0, rows, CHUNK):
                here = slice(r, r + CHUNK)
                image[p, here, :] += hist[t + 1, p, here, :] * laps[at_lap, p, here, :]
        return carry

    def start_copy(g, d):
        return pltpu.make_async_remote_copy(
            src_ref=stage.at[g], dst_ref=st_o.at[0, :, :, mine, :],
            send_sem=st_send.at[g], recv_sem=st_recv.at[d],
            device_id={"tm": g}, device_id_type=pl.DeviceIdType.MESH)

    def own_copy(g):
        return pltpu.make_async_copy(stage.at[g], st_o.at[0, :, :, mine, :], st_send.at[g])

    def send_start(g):
        end = tab[2 * steps + groups + g]
        for p in range(planes):
            stage[g, 0, p] = hist[end + 1, p]
            stage[g, 1, p] = hist[end, p]
        for m in range(groups):
            @pl.when(me == m)
            def _():
                if m == g:
                    own_copy(g).start()
                else:
                    start_copy(g, (m - g) % groups).start()

    done = 0
    for g in reversed(range(groups)):
        until = min(steps, (groups - g) * SLAB_MAX) if g > 0 else steps
        if until > done:
            lax.fori_loop(done, until, adjoint, 0)
            done = until
        send_start(g)

    def image_copy(i):
        return pltpu.make_async_remote_copy(
            src_ref=image, dst_ref=img_o.at[:, mine, :],
            send_sem=im_send.at[i], recv_sem=im_recv.at[i],
            device_id={"tm": partners[i]}, device_id_type=pl.DeviceIdType.MESH)

    for i in range(len(partners)):
        image_copy(i).start()
    own_image = pltpu.make_async_copy(image, img_o.at[:, mine, :], load_sem.at[0])
    own_image.start()

    for i in range(len(partners)):
        ck_copy(i).wait_send()
    for g in range(groups):
        for m in range(groups):
            @pl.when(me == m)
            def _():
                if m == g:
                    own_copy(g).wait()
                    for d in range(1, groups):
                        start_copy(g, d).wait_recv()
                else:
                    start_copy(g, (m - g) % groups).wait_send()
    for i in range(len(partners)):
        image_copy(i).wait()
    own_image.wait()


def run(steps, number, speed_sq, misfit_weight, checkpoints, adjoint_final, slab_steps, restart_group):
    planes, ny, nz = speed_sq.shape
    groups = slab_steps.shape[0]
    rows = ny // groups
    f32 = jnp.float32
    ends = jnp.cumsum(slab_steps[::-1])[::-1]
    begins = ends - slab_steps
    t = jnp.arange(steps)[:, None]
    inside = (t >= begins[None]) & (t < ends[None])
    n = slab_steps[None] - (t - begins[None])
    g = jnp.arange(groups)[None]
    some = jnp.any(inside, axis=1)
    at_u = jnp.sum(jnp.where(inside, (n + 1) * groups + g, 0), axis=1)
    at_lap = jnp.where(some, jnp.sum(jnp.where(inside, (n - 1) * groups + g, 0), axis=1), SLAB_MAX * groups)
    at_u = jnp.where(some, at_u, groups)
    table = jnp.concatenate([at_u, at_lap, restart_group, ends]).astype(jnp.int32)
    anywhere = pl.BlockSpec(memory_space=pl.ANY)
    padded = (planes + 2, rows + 2 * EDGE, nz)
    block = (planes, rows, nz)
    dma = pltpu.SemaphoreType.DMA
    return pl.pallas_call(
        functools.partial(kernel, steps),
        out_shape=(jax.ShapeDtypeStruct(speed_sq.shape, f32),
                   jax.ShapeDtypeStruct((1, 2) + speed_sq.shape, f32)),
        in_specs=[pl.BlockSpec(memory_space=pltpu.SMEM)] + [anywhere] * 4,
        out_specs=(anywhere, anywhere),
        scratch_shapes=[
            pltpu.VMEM((groups, 2) + block, f32),
            pltpu.VMEM(((SLAB_MAX + 2) * groups,) + padded, f32),
            pltpu.VMEM((SLAB_MAX * groups + 1,) + block, f32),
            pltpu.VMEM((2,) + padded, f32),
            pltpu.VMEM((steps + 2,) + block, f32),
            pltpu.VMEM(block, f32),
            pltpu.VMEM(block, f32),
            pltpu.VMEM(block, f32),
            pltpu.VMEM((groups, 2) + block, f32),
            dma((5,)), dma((groups - 1,)), dma((groups - 1,)),
            dma((2, groups, 4)), dma((2, groups, 4)), dma((2, 4)), dma((2, 4)),
            dma((groups,)), dma((groups,)), dma((groups - 1,)), dma((groups - 1,)),
        ],
        compiler_params=pltpu.CompilerParams(
            collective_id=number, has_side_effects=True, vmem_limit_bytes=56 * 1024 * 1024),
        name=f"wave{steps}",
    )(table, speed_sq, misfit_weight, checkpoints, adjoint_final)


def shards(*args):
    return run(SLAB_MAX * args[4].shape[0], 0, *args)


def solution(mesh):
    placed = (
        P("space", None, None),
        P("space", None, None),
        P("tm", None, "space", None, None),
        P(None, "space", None, None),
        P(),
        P(),
    )
    return jax.shard_map(
        shards,
        mesh=mesh,
        in_specs=placed,
        out_specs=(P("space", None, None), P("tm", None, "space", None, None)),
        check_vma=False,
    )
```

time: 811 us -> 218 us (0.27)
  waiting for transfers between devices: 340 us -> 0 us
  starting transfers between devices: 226 us -> 0 us
  Pallas kernels: 0 us -> 210 us
  other arithmetic: 172 us -> 2.93 us
  local copies, waits for them, and re-layouts: 37 us -> 4.6 us
  loops' own time: 15.7 us -> 0 us
  between operations: 16.3 us -> 0.65 us
    ppermute x63 -> x0, starting transfers between devices: 226 us -> none  [the longest x30 184 us: extended(): before = lax.ppermute(last, axis, up)]
    pallas_call x0 -> x1, Pallas kernels: none -> 210 us  [run(): pl.pallas_call(functools.partial(kernel, steps), out_shape=(jax.ShapeDtyp...]
    ppermute x63 -> x0, waiting for transfers between devices: 196 us -> none  [the longest x3 139 us: passed_along(): lax.ppermute(value, axis, [(source, source + steps) for source in range(i...]
    select_n x28 -> x1, other arithmetic: 109 us -> 0.01 us  [run(): at_u = jnp.where(some, at_u, groups)]
    all_gather x1 -> x0, waiting for transfers between devices: 89.7 us -> none  [shards(): stored = lax.all_gather(checkpoints, 'tm', axis=0, tiled=True)]
    psum x1 -> x0, waiting for transfers between devices: 53 us -> none  [shards(): total = lax.psum(image, 'tm')]
    mul x24 -> x0, other arithmetic: 32.6 us -> none  [one_step(): speed_sq * adj_now]
    slice x30 -> x0, local copies, waits for them, and re-layouts: 21.7 us -> none  [extended(): initial = lax.slice_in_dim(shard, 0, width, axis=dim)]
  transfers between devices with their start and end apart: 65 -> 0, of which waited for: 33 -> 0; matrix products, arithmetic and copies ran while one was open for 1% -> 0% of each run, Pallas kernels for 0% -> 0%
where the time goes in v1:
time: 218 us
  Pallas kernels  210 us (96%)
  local copies, waits for them, and re-layouts  4.6 us (2%)
  other arithmetic  2.93 us (1%)
    pallas_call x1, Pallas kernels, run(): pl.pallas_call(functools.partial(kernel, steps), out_shape=(jax.ShapeDtyp...  210 us

profile of v1, /device:TPU:0, one launch (start us, length us, event | category | flops | bytes accessed | tf_op | source)
XLA Modules:
  0.0 218.2 jit_solution(14295142102519420626)
XLA Ops:
  0.6 0.7 rev.6
  1.4 0.2 reduce-window.9
  1.6 0.1 rev.7
  1.7 0.7 sub.10
  2.3 0.1 fusion.1
  2.4 0.7 select_reduce_fusion.1
  3.2 1.2 pad_add_fusion.tab
  4.4 210.0 %wave24.1 = (f32[4,256,256]{2,1,0:T(8,128)}, f32[1,2,4,256,256]{4,3,2,1,0:T(8,128)}) custom-call(s32[56]{0:T(128)} %pad_add_fusion.tab, f32[4,256,256]{2,1,0:T(8,128)} %speed_h.1, f32[4,256,256]{2,1,0:T(8,128)} %weight_h.1, f32[1,2,4,256,256]{4,3,2,1,0:T(8,128)} %ck_h.1, f32[2,4,256,256]{3,2,1,0:T(8,128)} %af_h.1), custom_call_target="tpu_custom_call" | custom-call | tf_op jit(solution)/shard_map/wave24/pallas_call | solution.py:290
  214.4 0.0 copy-start
  214.4 2.4 %copy.10 = f32[4,256,256]{2,1,0:T(8,128)} copy(f32[4,256,256]{2,1,0:T(8,128)} %get-tuple-element.8) | data formatting | bytes 2097152
  216.8 0.0 copy-done
  216.8 1.3 copy.11
  (1 shorter events, 0.0 us)
Async XLA Ops:
  214.4 2.4 %copy-start = (f32[1,2,4,256,256]{4,3,2,1,0:T(8,128)S(1)}, f32[1,2,4,256,256]{4,3,2,1,0:T(8,128)}, u32[]{:S(2)}) copy-start(f32[1,2,4,256,256]{4,3,2,1,0:T(8,128)} %get-tuple-element.9) | copy-start | bytes 6291460

commit v2 on v1

--- a/solution.py
+++ b/solution.py
@@ -9,15 +9,17 @@
 
 SLAB_MAX = 6
 CHUNK = 32
+WIDE = 40
 EDGE = 8
 
 
 def kernel(steps, tab, speed_h, weight_h, ck_h, af_h, img_o, st_o,
            ck, u, laps, s, hist, image, spd, wgt, stage,
-           load_sem, ck_send, ck_recv, f_send, f_recv, a_send, a_recv,
+           yin, y_send, y_recv, load_sem, ck_send, ck_recv, f_send, f_recv, a_send, a_recv,
            st_send, st_recv, im_send, im_recv):
     groups = st_recv.shape[0]
-    planes, rows, _ = spd.shape
+    planes, rows, nz = image.shape
+    wide = rows + 2 * EDGE
     me = lax.axis_index("tm")
     sp = lax.axis_index("space")
     n_tm = lax.axis_size("tm")
@@ -36,10 +38,11 @@
               {"tm": place(jnp.maximum(q - 1, 0))}, {"tm": place(jnp.minimum(q + 1, n_tm - 1))}]
 
     def halo(d, ref, at, send, recv):
+        span_y = pl.ds(EDGE, ref.shape[2] - 2 * EDGE)
         if d == 0:
-            src, dst = ref.at[at, 1, inner, :], ref.at[at, planes + 1, inner, :]
+            src, dst = ref.at[at, 1, span_y, :], ref.at[at, planes + 1, span_y, :]
         elif d == 1:
-            src, dst = ref.at[at, planes, inner, :], ref.at[at, 0, inner, :]
+            src, dst = ref.at[at, planes, span_y, :], ref.at[at, 0, span_y, :]
         elif d == 2:
             src, dst = ref.at[at, span, pl.ds(EDGE, EDGE), :], ref.at[at, span, pl.ds(EDGE + rows, EDGE), :]
         else:
@@ -54,26 +57,34 @@
             def _():
                 halo(d, ref, at, sems[0](d), sems[1](d)).start()
 
-    def finish(ref, at, sems):
-        for d in range(4):
+    def finish(dirs, ref, at, sems):
+        for d in dirs:
             @pl.when(has[opposite[d]])
             def _():
                 halo(d, ref, at, sems[0](d), sems[1](d)).wait_recv()
-        for d in range(4):
+        for d in dirs:
             @pl.when(has[d])
             def _():
                 halo(d, ref, at, sems[0](d), sems[1](d)).wait_send()
 
     mine = pl.ds(pl.multiple_of(q * rows, rows), rows)
-    loads = [
-        pltpu.make_async_copy(speed_h.at[:, mine, :], spd, load_sem.at[0]),
-        pltpu.make_async_copy(weight_h.at[:, mine, :], wgt, load_sem.at[1]),
-        pltpu.make_async_copy(af_h.at[0, :, mine, :], hist.at[1], load_sem.at[2]),
-        pltpu.make_async_copy(af_h.at[1, :, mine, :], hist.at[0], load_sem.at[3]),
-        pltpu.make_async_copy(ck_h.at[0, :, :, mine, :], ck.at[me], load_sem.at[4]),
-    ]
+    loads = [pltpu.make_async_copy(ck_h.at[0, :, :, mine, :], ck.at[me], load_sem.at[0, 0])]
+    fields = [(speed_h, spd), (weight_h, wgt), (af_h.at[0], hist.at[1]), (af_h.at[1], hist.at[0])]
+    below = pl.ds(pl.multiple_of(jnp.maximum(q * rows - EDGE, 0), EDGE), EDGE)
+    above = pl.ds(pl.multiple_of(jnp.minimum(q * rows + rows, n_tm * rows - EDGE), EDGE), EDGE)
+    edges = []
+    for i, (src, dst) in enumerate(fields):
+        loads.append(pltpu.make_async_copy(src.at[:, mine, :], dst.at[:, inner, :], load_sem.at[1 + i, 0]))
+        edges.append((has[2], dst, 0, pltpu.make_async_copy(
+            src.at[:, below, :], dst.at[:, pl.ds(0, EDGE), :], load_sem.at[1 + i, 1])))
+        edges.append((has[3], dst, EDGE + rows, pltpu.make_async_copy(
+            src.at[:, above, :], dst.at[:, pl.ds(EDGE + rows, EDGE), :], load_sem.at[1 + i, 2])))
     for one in loads:
         one.start()
+    for there, _, _, one in edges:
+        @pl.when(there)
+        def _():
+            one.start()
 
     barrier = pltpu.get_barrier_semaphore()
     for m in partners:
@@ -96,45 +107,56 @@
     for i in range(len(partners)):
         ck_copy(i).start()
 
-    line = jnp.zeros((rows, spd.shape[2]), jnp.float32)
-    band = jnp.zeros((EDGE, spd.shape[2]), jnp.float32)
+    line = jnp.zeros((rows, nz), jnp.float32)
+    band = jnp.zeros((EDGE, nz), jnp.float32)
     for ref in (u, s):
         for d, p in ((0, 0), (1, planes + 1)):
             @pl.when(jnp.logical_not(has[d]))
             def _():
                 def clear(i, c):
-                    ref[i, p, EDGE:EDGE + rows, :] = line
+                    for r in range(EDGE, ref.shape[2] - EDGE, EDGE):
+                        ref[i, p, r:r + EDGE, :] = band
                     return c
                 lax.fori_loop(0, ref.shape[0], clear, 0)
-        for d, r in ((2, 0), (3, EDGE + rows)):
-            @pl.when(jnp.logical_not(has[d]))
-            def _():
-                def clear(i, c):
-                    for p in range(planes):
-                        ref[i, 1 + p, r:r + EDGE, :] = band
-                    return c
-                lax.fori_loop(0, ref.shape[0], clear, 0)
+    for d, r in ((2, 0), (3, EDGE + rows)):
+        @pl.when(jnp.logical_not(has[d]))
+        def _():
+            def clear(i, c):
+                for p in range(planes):
+                    u[i, 1 + p, r:r + EDGE, :] = band
+                return c
+            lax.fori_loop(0, u.shape[0], clear, 0)
+    for i in range(2):
+        for p in range(planes):
+            s[i, 1 + p, 0:EDGE, :] = band
+            s[i, 1 + p, EDGE + wide:2 * EDGE + wide, :] = band
+    for there, dst, r, _ in edges:
+        @pl.when(jnp.logical_not(there))
+        def _():
+            for p in range(planes):
+                dst[p, r:r + EDGE, :] = band
     blank = laps.shape[0] - 1
     for p in range(planes):
         laps[blank, p] = line
         image[p] = line
 
-    lane = lax.broadcasted_iota(jnp.int32, (CHUNK, spd.shape[2]), 1)
-    first = lane == 0
-    last = lane == spd.shape[2] - 1
-    zero = jnp.zeros((CHUNK, spd.shape[2]), jnp.float32)
-
-    def lap(ref, at, p, r):
-        c = ref[at, p + 1, EDGE + r:EDGE + r + CHUNK, :]
-        total = ref[at, p, EDGE + r:EDGE + r + CHUNK, :] + ref[at, p + 2, EDGE + r:EDGE + r + CHUNK, :]
-        total += ref[at, p + 1, EDGE + r - 1:EDGE + r - 1 + CHUNK, :]
-        total += ref[at, p + 1, EDGE + r + 1:EDGE + r + 1 + CHUNK, :]
-        total += jnp.where(first, zero, pltpu.roll(c, 1, 1))
-        total += jnp.where(last, zero, pltpu.roll(c, c.shape[1] - 1, 1))
+    def lap(ref, at, p, r, size):
+        lane = lax.broadcasted_iota(jnp.int32, (size, nz), 1)
+        zero = jnp.zeros((size, nz), jnp.float32)
+        c = ref[at, p + 1, EDGE + r:EDGE + r + size, :]
+        total = ref[at, p, EDGE + r:EDGE + r + size, :] + ref[at, p + 2, EDGE + r:EDGE + r + size, :]
+        total += ref[at, p + 1, EDGE + r - 1:EDGE + r - 1 + size, :]
+        total += ref[at, p + 1, EDGE + r + 1:EDGE + r + 1 + size, :]
+        total += jnp.where(lane == 0, zero, pltpu.roll(c, 1, 1))
+        total += jnp.where(lane == nz - 1, zero, pltpu.roll(c, nz - 1, 1))
         return c, total - 6.0 * c
 
     for one in loads:
         one.wait()
+    for there, _, _, one in edges:
+        @pl.when(there)
+        def _():
+            one.wait()
 
     def a_sems(par):
         return (lambda d: a_send.at[par, d]), (lambda d: a_recv.at[par, d])
@@ -143,7 +165,7 @@
         return (lambda d: f_send.at[par, g, d]), (lambda d: f_recv.at[par, g, d])
 
     for p in range(planes):
-        s[0, 1 + p, EDGE:EDGE + rows, :] = spd[p] * hist[1, p]
+        s[0, 1 + p, EDGE:EDGE + wide, :] = spd[p] * hist[1, p]
 
     for i in range(len(partners)):
         ck_copy(i).wait_recv()
@@ -154,7 +176,7 @@
         start(range(4), u, groups + g, f_sems(0, g))
         for p in range(planes):
             u[g, 1 + p, EDGE:EDGE + rows, :] = ck[source, 0, p]
-    start(range(4), s, 0, a_sems(0))
+    start((0, 1), s, 0, a_sems(0))
 
     order = (0, planes - 1) + tuple(range(1, planes - 1))
 
@@ -162,52 +184,79 @@
         par, later = lax.rem(n, 2), lax.rem(n + 1, 2)
         for g in range(groups):
             at = (n + 1) * groups + g
-            finish(u, at, f_sems(par, g))
+            finish(range(4), u, at, f_sems(par, g))
             for k, p in enumerate(order):
                 for r in range(0, rows, CHUNK):
                     here = slice(EDGE + r, EDGE + r + CHUNK)
-                    c, laplace = lap(u, at, p, r)
+                    c, laplace = lap(u, at, p, r, CHUNK)
                     laps[n * groups + g, p, r:r + CHUNK, :] = laplace
                     u[at + groups, 1 + p, here, :] = (
-                        2.0 * c - u[at - groups, 1 + p, here, :] + spd[p, r:r + CHUNK, :] * laplace)
+                        2.0 * c - u[at - groups, 1 + p, here, :] + spd[p, here, :] * laplace)
                 if k == 1:
                     @pl.when(n < SLAB_MAX - 1)
                     def _():
                         start((0, 1), u, at + groups, f_sems(later, g))
 
-            @pl.when(n < SLAB_MAX - 1)
-            def _():
-                start((2, 3), u, at + groups, f_sems(later, g))
+            start((2, 3), u, at + groups, f_sems(later, g))
         return carry
 
     lax.fori_loop(0, SLAB_MAX, forward, 0)
+    for g in range(groups):
+        finish((2, 3), u, (SLAB_MAX + 1) * groups + g, f_sems(SLAB_MAX % 2, g))
 
     def adjoint(t, carry):
         par, later = lax.rem(t, 2), lax.rem(t + 1, 2)
         at_u, at_lap = tab[t], tab[steps + t]
-        finish(s, par, a_sems(par))
+        finish((0, 1), s, par, a_sems(par))
         for k, p in enumerate(order):
-            for r in range(0, rows, CHUNK):
-                here = slice(r, r + CHUNK)
-                pad = slice(EDGE + r, EDGE + r + CHUNK)
-                _, laplace = lap(s, par, p, r)
+            for r in range(0, wide, WIDE):
+                here = slice(r, r + WIDE)
+                pad = slice(EDGE + r, EDGE + r + WIDE)
+                _, laplace = lap(s, par, p, r, WIDE)
                 new = (2.0 * hist[t + 1, p, here, :] - hist[t, p, here, :] + laplace
-                       + wgt[p, here, :] * u[at_u, 1 + p, pad, :])
+                       + wgt[p, here, :] * u[at_u, 1 + p, here, :])
                 hist[t + 2, p, here, :] = new
                 s[later, 1 + p, pad, :] = spd[p, here, :] * new
             if k == 1:
-                @pl.when(t < steps - 1)
+                @pl.when(jnp.logical_and(t < steps - 1, lax.rem(t + 1, EDGE) != 0))
                 def _():
                     start((0, 1), s, later, a_sems(later))
-
-        @pl.when(t < steps - 1)
-        def _():
-            start((2, 3), s, later, a_sems(later))
         for p in range(planes):
             for r in range(0, rows, CHUNK):
                 here = slice(r, r + CHUNK)
-                image[p, here, :] += hist[t + 1, p, here, :] * laps[at_lap, p, here, :]
+                image[p, here, :] += (hist[t + 1, p, EDGE + r:EDGE + r + CHUNK, :]
+                                      * laps[at_lap, p, here, :])
         return carry
+
+    def y_copy(t, k, d):
+        first = EDGE if d == 2 else rows
+        return pltpu.make_async_remote_copy(
+            src_ref=hist.at[pl.ds(t, 2), :, pl.ds(first, EDGE), :], dst_ref=yin.at[k, d - 2],
+            send_sem=y_send.at[k, d - 2], recv_sem=y_recv.at[k, d - 2],
+            device_id=target[d], device_id_type=pl.DeviceIdType.MESH)
+
+    def refresh(t):
+        k, par = t // EDGE - 1, t % 2
+        for d in (2, 3):
+            @pl.when(has[d])
+            def _():
+                y_copy(t, k, d).start()
+        for d in (2, 3):
+            r = 0 if d == 3 else EDGE + rows
+
+            @pl.when(has[opposite[d]])
+            def _():
+                y_copy(t, k, d).wait_recv()
+                for p in range(planes):
+                    old, now = yin[k, d - 2, 0, p], yin[k, d - 2, 1, p]
+                    hist[t, p, r:r + EDGE, :] = old
+                    hist[t + 1, p, r:r + EDGE, :] = now
+                    s[par, 1 + p, EDGE + r:2 * EDGE + r, :] = spd[p, r:r + EDGE, :] * now
+        start((0, 1), s, par, a_sems(par))
+        for d in (2, 3):
+            @pl.when(has[d])
+            def _():
+                y_copy(t, k, d).wait_send()
 
     def start_copy(g, d):
         return pltpu.make_async_remote_copy(
@@ -221,8 +270,8 @@
     def send_start(g):
         end = tab[2 * steps + groups + g]
         for p in range(planes):
-            stage[g, 0, p] = hist[end + 1, p]
-            stage[g, 1, p] = hist[end, p]
+            stage[g, 0, p] = hist[end + 1, p, EDGE:EDGE + rows, :]
+            stage[g, 1, p] = hist[end, p, EDGE:EDGE + rows, :]
         for m in range(groups):
             @pl.when(me == m)
             def _():
@@ -234,9 +283,12 @@
     done = 0
     for g in reversed(range(groups)):
         until = min(steps, (groups - g) * SLAB_MAX) if g > 0 else steps
-        if until > done:
-            lax.fori_loop(done, until, adjoint, 0)
-            done = until
+        while done < until:
+            stop = min(until, (done // EDGE + 1) * EDGE)
+            lax.fori_loop(done, stop, adjoint, 0)
+            done = stop
+            if done % EDGE == 0 and done < steps:
+                refresh(done)
         send_start(g)
 
     def image_copy(i):
@@ -247,7 +299,7 @@
 
     for i in range(len(partners)):
         image_copy(i).start()
-    own_image = pltpu.make_async_copy(image, img_o.at[:, mine, :], load_sem.at[0])
+    own_image = pltpu.make_async_copy(image, img_o.at[:, mine, :], load_sem.at[0, 0])
     own_image.start()
 
     for i in range(len(partners)):
@@ -286,6 +338,8 @@
     anywhere = pl.BlockSpec(memory_space=pl.ANY)
     padded = (planes + 2, rows + 2 * EDGE, nz)
     block = (planes, rows, nz)
+    tall = (planes, rows + 2 * EDGE, nz)
+    turns = max(1, (steps - 1) // EDGE)
     dma = pltpu.SemaphoreType.DMA
     return pl.pallas_call(
         functools.partial(kernel, steps),
@@ -297,13 +351,15 @@
             pltpu.VMEM((groups, 2) + block, f32),
             pltpu.VMEM(((SLAB_MAX + 2) * groups,) + padded, f32),
             pltpu.VMEM((SLAB_MAX * groups + 1,) + block, f32),
-            pltpu.VMEM((2,) + padded, f32),
-            pltpu.VMEM((steps + 2,) + block, f32),
+            pltpu.VMEM((2, planes + 2, rows + 4 * EDGE, nz), f32),
+            pltpu.VMEM((steps + 2,) + tall, f32),
             pltpu.VMEM(block, f32),
-            pltpu.VMEM(block, f32),
-            pltpu.VMEM(block, f32),
+            pltpu.VMEM(tall, f32),
+            pltpu.VMEM(tall, f32),
             pltpu.VMEM((groups, 2) + block, f32),
-            dma((5,)), dma((groups - 1,)), dma((groups - 1,)),
+            pltpu.VMEM((turns, 2, 2, planes, EDGE, nz), f32),
+            dma((turns, 2)), dma((turns, 2)),
+            dma((5, 3)), dma((groups - 1,)), dma((groups - 1,)),
             dma((2, groups, 4)), dma((2, groups, 4)), dma((2, 4)), dma((2, 4)),
             dma((groups,)), dma((groups,)), dma((groups - 1,)), dma((groups - 1,)),
         ],

time: 218 us -> 194 us (0.89)
  Pallas kernels: 210 us -> 185 us
    pallas_call x1, Pallas kernels: 210 us -> 185 us  [run(): pl.pallas_call(functools.partial(kernel, steps), out_shape=(jax.ShapeDtyp...]
where the time goes in v2:
time: 194 us; the launch traced here: 193 us
  Pallas kernels  185 us (95%)
  local copies, waits for them, and re-layouts  4.6 us (2%)
  other arithmetic  2.93 us (2%)
    pallas_call x1, Pallas kernels, run(): pl.pallas_call(functools.partial(kernel, steps), out_shape=(jax.ShapeDtyp...  185 us

profile of v2, /device:TPU:0, one launch (start us, length us, event | category | flops | bytes accessed | tf_op | source)
XLA Modules:
  0.0 193.3 jit_solution(4873846797025240927)
XLA Ops:
  0.6 0.7 rev.6
  1.4 0.2 reduce-window.9
  1.6 0.1 rev.7
  1.7 0.7 sub.10
  2.3 0.1 fusion.1
  2.4 0.7 select_reduce_fusion.1
  3.2 1.2 pad_add_fusion.tab
  4.4 185.1 %wave24.1 = (f32[4,256,256]{2,1,0:T(8,128)}, f32[1,2,4,256,256]{4,3,2,1,0:T(8,128)}) custom-call(s32[56]{0:T(128)} %pad_add_fusion.tab, f32[4,256,256]{2,1,0:T(8,128)} %speed_h.1, f32[4,256,256]{2,1,0:T(8,128)} %weight_h.1, f32[1,2,4,256,256]{4,3,2,1,0:T(8,128)} %ck_h.1, f32[2,4,256,256]{3,2,1,0:T(8,128)} %af_h.1), custom_call_target="tpu_custom_call" | custom-call | tf_op jit(solution)/shard_map/wave24/pallas_call | solution.py:344
  189.5 0.0 copy-start
  189.6 2.4 %copy.10 = f32[4,256,256]{2,1,0:T(8,128)} copy(f32[4,256,256]{2,1,0:T(8,128)} %get-tuple-element.8) | data formatting | bytes 2097152
  192.0 0.0 copy-done
  192.0 1.3 copy.11
  (1 shorter events, 0.0 us)
Async XLA Ops:
  189.5 2.4 %copy-start = (f32[1,2,4,256,256]{4,3,2,1,0:T(8,128)S(1)}, f32[1,2,4,256,256]{4,3,2,1,0:T(8,128)}, u32[]{:S(2)}) copy-start(f32[1,2,4,256,256]{4,3,2,1,0:T(8,128)} %get-tuple-element.9) | copy-start | bytes 6291460
